TPU v7x, 32 devices: a whole 2x2x4 slice. The times are simulated.
32 devices in a mesh: dp: 8 (over z, x), tensor: 4 (over y, core).
Axes of the slice: x: 2, y: 2, z: 4, core: 2. Of those that a mesh axis runs over, the one named last changes fastest.
Arguments:
- hidden_in: bfloat16 [16384, 640], P('dp'), may hold values from -6 to 6
- query_weight: bfloat16 [640, 1024], P(None, 'tensor'), may hold values from -0.25 to 0.25
- key_weight: bfloat16 [640, 256], replicated, may hold values from -0.25 to 0.25
- value_weight: bfloat16 [640, 256], replicated, may hold values from -0.25 to 0.25
- output_weight: bfloat16 [1024, 640], P('tensor'), may hold values from -0.1875 to 0.1875
- gate_weight: bfloat16 [640, 2048], P(None, 'tensor'), may hold values from -0.25 to 0.25
- up_weight: bfloat16 [640, 2048], P(None, 'tensor'), may hold values from -0.25 to 0.25
- down_weight: bfloat16 [2048, 640], P('tensor'), may hold values from -0.125 to 0.125
- pre_attention: float32 [640], replicated, may hold values from -0.5 to 0.5
- query_norm: float32 [256], replicated, may hold values from -0.5 to 0.5
- key_norm: float32 [256], replicated, may hold values from -0.5 to 0.5
- post_attention: float32 [640], replicated, may hold values from -0.5 to 0.5
- pre_feedforward: float32 [640], replicated, may hold values from -0.5 to 0.5
- post_feedforward: float32 [640], replicated, may hold values from -0.5 to 0.5
- segments: int32 [16384], P('dp'), may hold values from 0 to 15, as said below
- positions: int32 [16384], P('dp'), may hold values from 0 to 511, as said below
- cotangent: bfloat16 [16384, 640], P('dp'), may hold values from -6 to 6
Outputs:
- hidden_out: bfloat16 [16384, 640], P('dp')
- grad_input: float32 [16384, 640], P('dp')
- grad_query_weight: float32 [640, 1024], P(None, 'tensor')
- grad_key_weight: float32 [640, 256], replicated
- grad_value_weight: float32 [640, 256], replicated
- grad_output_weight: float32 [1024, 640], P('tensor')
- grad_gate_weight: float32 [640, 2048], P(None, 'tensor')
- grad_up_weight: float32 [640, 2048], P(None, 'tensor')
- grad_down_weight: float32 [2048, 640], P('tensor')
- grad_pre_attention: float32 [640], replicated
- grad_query_norm: float32 [256], replicated
- grad_key_norm: float32 [256], replicated
- grad_post_attention: float32 [640], replicated
- grad_pre_feedforward: float32 [640], replicated
- grad_post_feedforward: float32 [640], replicated
Inputs may be any that keep to these rules, and one draw needn't show every extreme that they name: `segments`: within each aligned block of 512 tokens the document numbers start at 0 at the block's first token and rise by 0 or 1 from one token to the next. `positions`: each token's position is its distance from the first token of its document in the same block.
All inputs are finite; a program needn't handle non-finite values.
Results may differ from a plain program's by a relative error of at most 0.02.
Values may be sent and summed in bfloat16 or wider, within the bound.
A program may use at most 128 MiB of HBM per device.

v0:
```python
import jax
import jax.numpy as jnp
from jax import lax
from jax.sharding import PartitionSpec as P

LEN = 512


epsilon = 1e-06
rope_base = 1000000.0
masked_score = -1e30


def normed(values, norm_gain):
    inverse = lax.rsqrt(jnp.mean(values * values, axis=-1, keepdims=True) + epsilon)
    return values * inverse * (1.0 + norm_gain)


def rotary(values, cosine, sine_table):
    half_width = values.shape[-1] // 2
    front_half = values[..., :half_width]
    second = values[..., half_width:]
    return jnp.concatenate(
        [front_half * cosine - second * sine_table, second * cosine + front_half * sine_table],
        axis=-1,
    )


def rotary_tables(positions, head_width):
    steps_half = jnp.arange(head_width // 2).astype(jnp.float32)
    frequency = jnp.power(jnp.float32(rope_base), -2.0 * steps_half / head_width)
    angles = positions.astype(jnp.float32)[:, None] * frequency[None, :]
    return (jnp.cos(angles), jnp.sin(angles))


def gated(gate_proj, up_proj):
    return jax.nn.gelu(gate_proj, approximate=True) * up_proj


def pack_mask(segment):
    offsets = jnp.arange(segment.shape[0])
    return (segment[:, None] == segment[None, :]) & (offsets[None, :] <= offsets[:, None])


def pack_scores(queries, key_rows, segment):
    score_scale = queries.shape[-1] ** (-0.5)
    scores = (
        jnp.einsum("ihd,jd->hij", queries, key_rows, preferred_element_type=jnp.float32)
        * score_scale
    )
    return jnp.where(pack_mask(segment)[None], scores, masked_score)


def attend_pack(inputs):
    queries, key_rows, values, segment = inputs
    scores = pack_scores(queries, key_rows, segment)
    top_score = jnp.max(scores, axis=-1, keepdims=True)
    log_total = top_score + jnp.log(jnp.sum(jnp.exp(scores - top_score), axis=-1, keepdims=True))
    prob_low = jnp.exp(scores - log_total).astype(jnp.bfloat16)
    mixture = jnp.einsum("hij,jd->ihd", prob_low, values, preferred_element_type=jnp.float32)
    return (mixture.astype(jnp.bfloat16), log_total)


def attend_back(inputs):
    queries, key_rows, values, segment, log_total, mixture_grad = inputs
    score_scale = queries.shape[-1] ** (-0.5)
    probability = jnp.exp(pack_scores(queries, key_rows, segment) - log_total)
    prob_low = probability.astype(jnp.bfloat16)
    value_grad = jnp.einsum(
        "hij,ihd->jhd", prob_low, mixture_grad, preferred_element_type=jnp.float32
    )
    prob_grad = jnp.einsum("ihd,jd->hij", mixture_grad, values, preferred_element_type=jnp.float32)
    row_terms = jnp.sum(probability * prob_grad, axis=-1, keepdims=True)
    score_grad = (probability * (prob_grad - row_terms)).astype(jnp.bfloat16)
    query_grad = (
        jnp.einsum("hij,jd->ihd", score_grad, key_rows, preferred_element_type=jnp.float32)
        * score_scale
    )
    key_grad = (
        jnp.einsum("hij,ihd->jhd", score_grad, queries, preferred_element_type=jnp.float32)
        * score_scale
    )
    return (query_grad, key_grad, value_grad.astype(jnp.bfloat16))


def run_layer(
    hidden_in,
    query_weight,
    key_weight,
    value_weight,
    output_weight,
    gate_weight,
    up_weight,
    down_weight,
    pre_attention,
    query_norm,
    key_norm,
    post_attention,
    pre_feedforward,
    post_feedforward,
    segments,
    positions,
    cotangent,
    reducers,
    feed_hook,
):
    attention_reduce, feed_reduce, feed_back_reduce, attention_back_reduce = reducers
    tokens = hidden_in.shape[0]
    pack_length = LEN
    pack_count = tokens // pack_length
    head_width = key_weight.shape[1]
    local_heads = query_weight.shape[1] // head_width
    hidden = hidden_in.astype(jnp.float32)
    cosine, sine_table = rotary_tables(positions, head_width)

    def head_path(projected, norm_gain):
        return rotary(normed(projected, norm_gain), cosine[:, None, :], sine_table[:, None, :])

    normed_value, pre_back = jax.vjp(normed, hidden, pre_attention)
    normed_in = normed_value.astype(jnp.bfloat16)
    query_proj = jnp.dot(normed_in, query_weight, preferred_element_type=jnp.float32)
    query_proj = query_proj.reshape(tokens, local_heads, head_width)
    key_proj = jnp.dot(normed_in, key_weight, preferred_element_type=jnp.float32)
    value_low = jnp.dot(normed_in, value_weight, preferred_element_type=jnp.float32).astype(
        jnp.bfloat16
    )
    query_rot, query_back = jax.vjp(head_path, query_proj, query_norm)
    key_heads = key_proj[:, None, :]
    key_rot, key_back = jax.vjp(head_path, key_heads, key_norm)
    query_packs = query_rot.astype(jnp.bfloat16).reshape(
        pack_count, pack_length, local_heads, head_width
    )
    key_packs = key_rot[:, 0, :].astype(jnp.bfloat16).reshape(pack_count, pack_length, head_width)
    value_packs = value_low.reshape(pack_count, pack_length, head_width)
    segment_packs = segments.reshape(pack_count, pack_length)
    mixture, log_total = lax.map(attend_pack, (query_packs, key_packs, value_packs, segment_packs))
    mixture_low = mixture.reshape(tokens, local_heads * head_width)
    attention = attention_reduce(
        jnp.dot(mixture_low, output_weight, preferred_element_type=jnp.float32)
    )
    post_value, post_att_back = jax.vjp(normed, attention, post_attention)
    middle = hidden + post_value
    mid_value, mid_back = jax.vjp(normed, middle, pre_feedforward)
    normed_mid = mid_value.astype(jnp.bfloat16)
    gate_proj = jnp.dot(normed_mid, gate_weight, preferred_element_type=jnp.float32)
    up_proj = jnp.dot(normed_mid, up_weight, preferred_element_type=jnp.float32)
    product, gated_back = jax.vjp(gated, gate_proj, up_proj)
    product_low = product.astype(jnp.bfloat16)
    feed = feed_reduce(jnp.dot(product_low, down_weight, preferred_element_type=jnp.float32))
    feed_value, feed_out_back = jax.vjp(normed, feed, post_feedforward)
    hidden_out = (middle + feed_value).astype(jnp.bfloat16)
    cotangent_full = cotangent.astype(jnp.float32)
    feed_grad, grad_post_feedforward = feed_out_back(cotangent_full)
    feed_grad_low = feed_grad.astype(jnp.bfloat16)
    grad_down_weight = jnp.einsum(
        "tf,td->fd", product_low, feed_grad_low, preferred_element_type=jnp.float32
    )
    product_grad = jnp.einsum(
        "td,fd->tf", feed_grad_low, down_weight, preferred_element_type=jnp.float32
    )
    gate_grad, up_grad = gated_back(product_grad)
    gate_grad_low = gate_grad.astype(jnp.bfloat16)
    up_grad_low = up_grad.astype(jnp.bfloat16)
    grad_gate_weight = jnp.einsum(
        "td,tf->df", normed_mid, gate_grad_low, preferred_element_type=jnp.float32
    )
    grad_up_weight = jnp.einsum(
        "td,tf->df", normed_mid, up_grad_low, preferred_element_type=jnp.float32
    )
    grad_gate_weight, grad_up_weight, grad_down_weight, grad_post_feedforward = feed_hook(
        (grad_gate_weight, grad_up_weight, grad_down_weight, grad_post_feedforward)
    )
    mid_part = jnp.einsum(
        "tf,df->td", gate_grad_low, gate_weight, preferred_element_type=jnp.float32
    )
    mid_part = mid_part + jnp.einsum(
        "tf,df->td", up_grad_low, up_weight, preferred_element_type=jnp.float32
    )
    mid_normed_grad = feed_back_reduce(mid_part)
    middle_part, grad_pre_feedforward = mid_back(mid_normed_grad)
    middle_grad = cotangent_full + middle_part
    attention_grad, grad_post_attention = post_att_back(middle_grad)
    attention_grad_low = attention_grad.astype(jnp.bfloat16)
    grad_output_weight = jnp.einsum(
        "tk,td->kd", mixture_low, attention_grad_low, preferred_element_type=jnp.float32
    )
    mixture_grad = jnp.einsum(
        "td,kd->tk", attention_grad_low, output_weight, preferred_element_type=jnp.float32
    )
    mixture_grad_packs = mixture_grad.astype(jnp.bfloat16).reshape(
        pack_count, pack_length, local_heads, head_width
    )
    query_rot_grad, key_rot_grad, value_grad_low = lax.map(
        attend_back,
        (query_packs, key_packs, value_packs, segment_packs, log_total, mixture_grad_packs),
    )
    query_grad, grad_query_norm = query_back(
        query_rot_grad.reshape(tokens, local_heads, head_width)
    )
    key_grad, grad_key_norm = key_back(key_rot_grad.reshape(tokens, local_heads, head_width))
    query_grad_low = query_grad.astype(jnp.bfloat16).reshape(tokens, local_heads * head_width)
    key_grad_low = key_grad.astype(jnp.bfloat16)
    value_grad_low = value_grad_low.reshape(tokens, local_heads, head_width)
    grad_query_weight = jnp.einsum(
        "td,tk->dk", normed_in, query_grad_low, preferred_element_type=jnp.float32
    )
    grad_key_weight = jnp.einsum(
        "td,thk->dk", normed_in, key_grad_low, preferred_element_type=jnp.float32
    )
    grad_value_weight = jnp.einsum(
        "td,thk->dk", normed_in, value_grad_low, preferred_element_type=jnp.float32
    )
    in_part = jnp.einsum(
        "tk,dk->td", query_grad_low, query_weight, preferred_element_type=jnp.float32
    )
    in_part = in_part + jnp.einsum(
        "thk,dk->td", key_grad_low, key_weight, preferred_element_type=jnp.float32
    )
    in_part = in_part + jnp.einsum(
        "thk,dk->td", value_grad_low, value_weight, preferred_element_type=jnp.float32
    )
    in_normed_grad = attention_back_reduce(in_part)
    input_part, grad_pre_attention = pre_back(in_normed_grad)
    grad_input = middle_grad + input_part
    return (
        hidden_out,
        grad_input,
        grad_query_weight,
        grad_key_weight,
        grad_value_weight,
        grad_output_weight,
        grad_gate_weight,
        grad_up_weight,
        grad_down_weight,
        grad_pre_attention,
        grad_query_norm,
        grad_key_norm,
        grad_post_attention,
        grad_pre_feedforward,
        grad_post_feedforward,
    )


def on_device(
    hidden_in,
    query_weight,
    key_weight,
    value_weight,
    output_weight,
    gate_weight,
    up_weight,
    down_weight,
    pre_attention,
    query_norm,
    key_norm,
    post_attention,
    pre_feedforward,
    post_feedforward,
    segments,
    positions,
    cotangent,
):

    def attention_reduce(values):
        return lax.psum(values, "tensor")

    def feed_reduce(values):
        return lax.psum(values.astype(jnp.bfloat16), "tensor").astype(jnp.float32)

    def feed_back_reduce(values):
        return lax.psum(values.astype(jnp.bfloat16), "tensor").astype(jnp.float32)

    def attention_back_reduce(values):
        return lax.psum(values.astype(jnp.bfloat16), "tensor").astype(jnp.float32)

    def feed_hook(grads):
        return grads

    (
        hidden_out,
        grad_input,
        grad_query_weight,
        grad_key_weight,
        grad_value_weight,
        grad_output_weight,
        grad_gate_weight,
        grad_up_weight,
        grad_down_weight,
        grad_pre_attention,
        grad_query_norm,
        grad_key_norm,
        grad_post_attention,
        grad_pre_feedforward,
        grad_post_feedforward,
    ) = run_layer(
        hidden_in,
        query_weight,
        key_weight,
        value_weight,
        output_weight,
        gate_weight,
        up_weight,
        down_weight,
        pre_attention,
        query_norm,
        key_norm,
        post_attention,
        pre_feedforward,
        post_feedforward,
        segments,
        positions,
        cotangent,
        (attention_reduce, feed_reduce, feed_back_reduce, attention_back_reduce),
        feed_hook,
    )
    grad_key_weight, grad_value_weight, grad_query_norm, grad_key_norm = lax.psum(
        (grad_key_weight, grad_value_weight, grad_query_norm, grad_key_norm), ("dp", "tensor")
    )
    (
        grad_query_weight,
        grad_output_weight,
        grad_gate_weight,
        grad_up_weight,
        grad_down_weight,
        grad_pre_attention,
        grad_post_attention,
        grad_pre_feedforward,
        grad_post_feedforward,
    ) = lax.psum(
        (
            grad_query_weight,
            grad_output_weight,
            grad_gate_weight,
            grad_up_weight,
            grad_down_weight,
            grad_pre_attention,
            grad_post_attention,
            grad_pre_feedforward,
            grad_post_feedforward,
        ),
        "dp",
    )
    return (
        hidden_out,
        grad_input,
        grad_query_weight,
        grad_key_weight,
        grad_value_weight,
        grad_output_weight,
        grad_gate_weight,
        grad_up_weight,
        grad_down_weight,
        grad_pre_attention,
        grad_query_norm,
        grad_key_norm,
        grad_post_attention,
        grad_pre_feedforward,
        grad_post_feedforward,
    )


def solution(mesh):
    placed = (
        P("dp", None),
        P(None, "tensor"),
        P(),
        P(),
        P("tensor", None),
        P(None, "tensor"),
        P(None, "tensor"),
        P("tensor", None),
        P(),
        P(),
        P(),
        P(),
        P(),
        P(),
        P("dp"),
        P("dp"),
        P("dp", None),
    )
    return jax.shard_map(
        on_device,
        mesh=mesh,
        in_specs=placed,
        out_specs=(
            P("dp", None),
            P("dp", None),
            P(None, "tensor"),
            P(),
            P(),
            P("tensor", None),
            P(None, "tensor"),
            P(None, "tensor"),
            P("tensor", None),
            P(),
            P(),
            P(),
            P(),
            P(),
            P(),
        ),
        check_vma=False,
    )
```

profile of v0, /device:TPU:0, one launch (start us, length us, event | category | flops | bytes accessed | tf_op | source)
XLA Modules:
  0.0 910.0 jit_solution(12823472843531258651)
XLA Ops:
  21.4 5.7 fusion.99
  43.3 26.9 %while.26 = (s32[]{:T(128)}, bf16[4,512,1,256]{3,1,0,2:T(8,128)(2,1)}, f32[4,1,512,1]{2,3,1,0:T(1,128)}, bf16[4,512,256]{2,1,0:T(8,128)(2,1)}, s32[4,512]{1,0:T(...) while((s32[]{:T(128)}, bf16[4,512,1,256]{3,1,0,2:T(8,128)(2,1)}, ...), condition=%wide.region_6.7_spmd, body=%wide.region_3.6_spmd.sunk | while | flops 271187456 | bytes 5272153 | solution.py:136
  70.2 4.6 fusion.115
  75.6 104.7 %all-reduce.15.cloned.1.call-done = f32[2048,640]{1,0:T(8,128)} async-done(((f32[2048,640]{1,0:T(8,128)}), f32[2048,640]{1,0:T(8,128)}) %all-reduce.15.cloned.1.call-update) | async-done | bytes 5242896 | tf_op jit(solution)/shard_map/psum | solution.py:265
  199.4 59.6 %all-reduce.17.cloned.1.call-done = bf16[2048,640]{1,0:T(8,128)(2,1)} async-done(((bf16[2048,640]{1,0:T(8,128)(2,1)}), bf16[2048,640]{1,0:T(8,128)(2,1)}) %all-reduce.17.cloned.1.call-update) | async-done | bytes 2621456 | tf_op jit(solution)/shard_map/psum | solution.py:268
  267.9 4.9 multiply_convert_fusion.2
  278.5 5.3 fusion.126
  283.7 54.6 %all-reduce.19.cloned.1.call-done = bf16[2048,640]{1,0:T(8,128)(2,1)} async-done(((bf16[2048,640]{1,0:T(8,128)(2,1)}), bf16[2048,640]{1,0:T(8,128)(2,1)}) %all-reduce.19.cloned.1.call-update) | async-done | bytes 2621456 | tf_op jit(solution)/shard_map/psum | solution.py:271
  343.1 7.7 multiply_reduce_fusion.1
  355.8 125.7 %while.27 = (s32[]{:T(128)}, f32[4,512,1,256]{1,0,3,2:T(4,128)}, f32[4,512,1,256]{1,0,3,2:T(4,128)}, bf16[4,512,1,256]{3,1,0,2:T(8,128)(2,1)}, bf16[4,512,256]{2...) while((s32[]{:T(128)}, f32[4,512,1,256]{1,0,3,2:T(4,128)}, ...), condition=%wide.region_18.19_spmd, body=%wide.region_16.18_spmd.sunk | while | flops 674627072 | bytes 16275081 | solution.py:193
  362.0 11.0 %dynamic_update_slice.30 = f32[4,512,1,256]{1,0,3,2:T(4,128)} dynamic-update-slice(f32[4,512,1,256]{1,0,3,2:T(4,128)} %get-tuple-element.387, f32[1,512,1,256]{1,0,3,2:T(1,128)S(1)} %copy.93, s32[]{:T(128)} %get-tuple-element.385, s32[]{:T(128)} %constant.83.clone.1..sunk, s32[]{:T(128)} %constant.83.clone.1..sunk, s32[]{:T(128)} %constant.83.clone.1..sunk) | dynamic-update-slice | bytes 1048580 | tf_op jit(solution)/shard_map/while/body/jit(dynamic_update_index_in_dim)/dynamic_update_slice | solution.py:193
  374.9 11.1 %dynamic_update_slice.29 = f32[4,512,1,256]{1,0,3,2:T(4,128)} dynamic-update-slice(f32[4,512,1,256]{1,0,3,2:T(4,128)} %get-tuple-element.386, f32[1,512,1,256]{1,0,3,2:T(1,128)S(1)} %copy.92, s32[]{:T(128)} %get-tuple-element.385, s32[]{:T(128)} %constant.83.clone.1..sunk, s32[]{:T(128)} %constant.83.clone.1..sunk, s32[]{:T(128)} %constant.83.clone.1..sunk) | dynamic-update-slice | bytes 1048580 | tf_op jit(solution)/shard_map/while/body/jit(dynamic_update_index_in_dim)/dynamic_update_slice | solution.py:193
  393.5 11.0 %dynamic_update_slice.30 = f32[4,512,1,256]{1,0,3,2:T(4,128)} dynamic-update-slice(f32[4,512,1,256]{1,0,3,2:T(4,128)} %get-tuple-element.387, f32[1,512,1,256]{1,0,3,2:T(1,128)S(1)} %copy.93, s32[]{:T(128)} %get-tuple-element.385, s32[]{:T(128)} %constant.83.clone.1..sunk, s32[]{:T(128)} %constant.83.clone.1..sunk, s32[]{:T(128)} %constant.83.clone.1..sunk) | dynamic-update-slice | bytes 1048580 | tf_op jit(solution)/shard_map/while/body/jit(dynamic_update_index_in_dim)/dynamic_update_slice | solution.py:193
  406.3 11.1 %dynamic_update_slice.29 = f32[4,512,1,256]{1,0,3,2:T(4,128)} dynamic-update-slice(f32[4,512,1,256]{1,0,3,2:T(4,128)} %get-tuple-element.386, f32[1,512,1,256]{1,0,3,2:T(1,128)S(1)} %copy.92, s32[]{:T(128)} %get-tuple-element.385, s32[]{:T(128)} %constant.83.clone.1..sunk, s32[]{:T(128)} %constant.83.clone.1..sunk, s32[]{:T(128)} %constant.83.clone.1..sunk) | dynamic-update-slice | bytes 1048580 | tf_op jit(solution)/shard_map/while/body/jit(dynamic_update_index_in_dim)/dynamic_update_slice | solution.py:193
  424.9 11.0 %dynamic_update_slice.30 = f32[4,512,1,256]{1,0,3,2:T(4,128)} dynamic-update-slice(f32[4,512,1,256]{1,0,3,2:T(4,128)} %get-tuple-element.387, f32[1,512,1,256]{1,0,3,2:T(1,128)S(1)} %copy.93, s32[]{:T(128)} %get-tuple-element.385, s32[]{:T(128)} %constant.83.clone.1..sunk, s32[]{:T(128)} %constant.83.clone.1..sunk, s32[]{:T(128)} %constant.83.clone.1..sunk) | dynamic-update-slice | bytes 1048580 | tf_op jit(solution)/shard_map/while/body/jit(dynamic_update_index_in_dim)/dynamic_update_slice | solution.py:193
  437.8 11.1 %dynamic_update_slice.29 = f32[4,512,1,256]{1,0,3,2:T(4,128)} dynamic-update-slice(f32[4,512,1,256]{1,0,3,2:T(4,128)} %get-tuple-element.386, f32[1,512,1,256]{1,0,3,2:T(1,128)S(1)} %copy.92, s32[]{:T(128)} %get-tuple-element.385, s32[]{:T(128)} %constant.83.clone.1..sunk, s32[]{:T(128)} %constant.83.clone.1..sunk, s32[]{:T(128)} %constant.83.clone.1..sunk) | dynamic-update-slice | bytes 1048580 | tf_op jit(solution)/shard_map/while/body/jit(dynamic_update_index_in_dim)/dynamic_update_slice | solution.py:193
  456.4 11.0 %dynamic_update_slice.30 = f32[4,512,1,256]{1,0,3,2:T(4,128)} dynamic-update-slice(f32[4,512,1,256]{1,0,3,2:T(4,128)} %get-tuple-element.387, f32[1,512,1,256]{1,0,3,2:T(1,128)S(1)} %copy.93, s32[]{:T(128)} %get-tuple-element.385, s32[]{:T(128)} %constant.83.clone.1..sunk, s32[]{:T(128)} %constant.83.clone.1..sunk, s32[]{:T(128)} %constant.83.clone.1..sunk) | dynamic-update-slice | bytes 1048580 | tf_op jit(solution)/shard_map/while/body/jit(dynamic_update_index_in_dim)/dynamic_update_slice | solution.py:193
  469.2 11.1 %dynamic_update_slice.29 = f32[4,512,1,256]{1,0,3,2:T(4,128)} dynamic-update-slice(f32[4,512,1,256]{1,0,3,2:T(4,128)} %get-tuple-element.386, f32[1,512,1,256]{1,0,3,2:T(1,128)S(1)} %copy.92, s32[]{:T(128)} %get-tuple-element.385, s32[]{:T(128)} %constant.83.clone.1..sunk, s32[]{:T(128)} %constant.83.clone.1..sunk, s32[]{:T(128)} %constant.83.clone.1..sunk) | dynamic-update-slice | bytes 1048580 | tf_op jit(solution)/shard_map/while/body/jit(dynamic_update_index_in_dim)/dynamic_update_slice | solution.py:193
  487.9 7.6 fusion.104
  523.1 40.2 %all-reduce.4 = (f32[256]{0:T(256)}, f32[256]{0:T(256)}) all-reduce(f32[256]{0:T(256)S(1)} %get-tuple-element.156, f32[256]{0:T(256)S(1)} %get-tuple-element.154), channel_id=1, replica_groups=mesh['dp'=8,'tensor'=4] {'dp','tensor'}, use_global_device_ids=true, to_apply=%region_33.34 | all-reduce | flops 512 | bytes 4096 | tf_op jit(solution)/shard_map/psum | solution.py:316
  570.4 37.7 %all-reduce.6 = (f32[640]{0:T(1024)}, f32[640]{0:T(1024)}, f32[640]{0:T(1024)}, f32[640]{0:T(1024)}) all-reduce(f32[640]{0:T(1024)S(1)} %get-tuple-element.152, f32[640]{0:T(1024)S(1)} %get-tuple-element.146, f32[640]{0:T(1024)S(1)} %get-tuple-element.148, f32[640]{0:T(1024)S(1)} %get-tuple-element.150), channel_id=1, replica_groups=mesh['dp'=8,'tensor'=4] {'dp'}, use_global_device_ids=true, to_apply=%region_31.32 | all-reduce | flops 2560 | bytes 20480 | tf_op jit(solution)/shard_map/psum | solution.py:329
  608.1 5.5 fusion.60
  613.6 90.6 %all-reduce.23.cloned.1.call-done = (f32[640,256]{1,0:T(8,128)}, f32[640,256]{1,0:T(8,128)}) async-done(((f32[640,256]{1,0:T(8,128)}, f32[640,256]{1,0:T(8,128)}), (f32[640,256]{1,0:T(8,128)}, f32[640,256]{1,0:T(8,128)})) %all-reduce.23.cloned.1.call-update) | async-done | bytes 1310736 | tf_op jit(solution)/shard_map/psum | solution.py:316
  704.2 189.8 %all-reduce.25.cloned.1.call-done = (f32[640,256]{1,0:T(8,128)}, f32[256,640]{1,0:T(8,128)}, f32[640,512]{1,0:T(8,128)}, f32[640,512]{1,0:T(8,128)}, f32[512,640]{1,0:T(8,128)}) async-done(((f32[640,256]{1,0:T(8,128)}, f32[256,640]{1,0:T(8,128)}, f32[640,512]{1,0:T(8,128)}, f32[640,512]{1,0:T(8,128)}, f32[512,640]{1,0:T(8,128)}), (f32[640,256]{1,0:T(8,128)}, f32[256,640]{1,0:T(8,128)}, ...) | async-done | bytes 5242896 | tf_op jit(solution)/shard_map/psum | solution.py:329
  (320 shorter events, 187.9 us)
Async XLA Ops:
  7.2 188.3 %copy-start = (bf16[512,640]{1,0:T(8,128)(2,1)S(1)}, bf16[512,640]{1,0:T(8,128)(2,1)}, u32[]{:S(2)}) copy-start(bf16[512,640]{1,0:T(8,128)(2,1)} %param.28) | copy-start | bytes 1966084
  7.2 173.1 %all-reduce.15.cloned.1.call-start = ((), (), s32[]{:S(2)}) async-start(), calls=%async_computation | async-start | bytes 10485760 | tf_op jit(solution)/shard_map/psum | solution.py:265
  7.3 14.1 %copy-start.66 = (f32[128]{0:T(128)}, f32[128]{0:T(128)S(1)}, u32[]{:S(2)}) copy-start(f32[128]{0:T(128)S(1)} %multiply_power_fusion) | copy-start | bytes 1540
  13.2 5.4 copy-start.46
  15.5 5.8 copy-start.54
  15.6 5.7 copy-start.44
  74.9 184.1 %all-reduce.17.cloned.1.call-start = ((), (), s32[]{:S(2)}) async-start(), calls=%async_computation.1 | async-start | bytes 5242880 | tf_op jit(solution)/shard_map/psum | solution.py:268
  198.8 139.5 %all-reduce.19.cloned.1.call-start = ((), (), s32[]{:S(2)}) async-start(), calls=%async_computation.2 | async-start | bytes 5242880 | tf_op jit(solution)/shard_map/psum | solution.py:271
  261.5 5.7 copy-start.73
  267.2 5.6 copy-start.27
  267.9 4.9 copy-start.37
  278.1 288.3 %all-reduce.21.cloned.1.call-start = ((), (), s32[]{:S(2)}) async-start(), calls=%async_computation.3 | async-start | bytes 5242880 | tf_op jit(solution)/shard_map/psum | solution.py:274
  342.7 8.2 slice-start
  343.1 7.8 slice-start.1
  487.9 7.6 copy-start.8
  487.9 7.6 copy-start.47
  487.9 7.6 copy-start.59
  505.0 199.2 %all-reduce.23.cloned.1.call-start = ((), (), s32[]{:S(2)}) async-start(), calls=%async_computation.4 | async-start | bytes 2621440 | tf_op jit(solution)/shard_map/psum | solution.py:316
  517.2 376.8 %all-reduce.25.cloned.1.call-start = ((), (), s32[]{:S(2)}) async-start(), calls=%async_computation.5 | async-start | bytes 10485760 | tf_op jit(solution)/shard_map/psum | solution.py:329
  523.1 43.3 %copy-start.5 = (bf16[2048,640]{1,0:T(8,128)(2,1)S(1)}, bf16[2048,640]{1,0:T(8,128)(2,1)}, u32[]{:S(2)}) copy-start(bf16[2048,640]{1,0:T(8,128)(2,1)} %param.21) | copy-start | bytes 7864324
  563.3 44.8 %copy-start.51 = (f32[2048]{0:T(1024)S(1)}, f32[2048]{0:T(1024)}, u32[]{:S(2)}) copy-start(f32[2048]{0:T(1024)} %copy-done.50) | copy-start | bytes 24580
  704.2 193.9 %copy-start.34 = (f32[640,256]{1,0:T(8,128)S(1)}, f32[640,256]{1,0:T(8,128)}, u32[]{:S(2)}) copy-start(f32[640,256]{1,0:T(8,128)} %get-tuple-element.413) | copy-start | bytes 1966084
  894.0 4.9 copy-start.35
  894.0 5.8 copy-start.33
  (58 other events, 139.5 us)
Sparse Core Ops, SparseCore 0:
  75.0 105.2 all-reduce.14
  198.9 60.0 all-reduce.16
  278.3 59.9 all-reduce.18
  505.1 61.2 all-reduce.20
  572.4 131.7 all-reduce.22
  709.5 184.4 all-reduce.24
where the time goes:
time: 920 us; the launch traced here: 910 us
  waiting for transfers between devices  502 us (55%)
  local copies, waits for them, and re-layouts  153 us (17%)
  matrix products  95.9 us (10%)
  blocking collectives  77.9 us (8%)
  other arithmetic  64 us (7%)
  between operations  15.1 us (2%)
    psum x1, waiting for transfers between devices, on_device(): lax.psum((grad_query_weight, grad_output_weight, grad_gate_weight, grad_u...  190 us
    psum x1, waiting for transfers between devices, attention_reduce(): return lax.psum(values, 'tensor')  105 us
    dynamic_update_slice x16, local copies, waits for them, and re-layouts, run_layer(): lax.map(attend_back, (query_packs, key_packs, value_packs, segment_packs,...  92.6 us
    psum x1, waiting for transfers between devices, on_device(): lax.psum((grad_key_weight, grad_value_weight, grad_query_norm, grad_key_n...  90.6 us
    psum x1, waiting for transfers between devices, feed_reduce(): return lax.psum(values.astype(jnp.bfloat16), 'tensor').astype(jnp.float32)  59.6 us
    psum x1, waiting for transfers between devices, feed_back_reduce(): return lax.psum(values.astype(jnp.bfloat16), 'tensor').astype(jnp.float32)  54.6 us
    psum x1, blocking collectives, on_device(): lax.psum((grad_key_weight, grad_value_weight, grad_query_norm, grad_key_n...  40.2 us
    psum x1, blocking collectives, on_device(): lax.psum((grad_query_weight, grad_output_weight, grad_gate_weight, grad_u...  37.7 us
  transfers between devices with their start and end apart: 6, of which 6 were waited for; matrix products, arithmetic and copies ran while one was open for 3% of the time, Pallas kernels for 0%

commit v1 on v0

v1 whole, which is shorter than its diff:
```python
import jax
import jax.numpy as jnp
from jax import lax
from jax.experimental import pallas as pl
from jax.experimental.pallas import tpu as pltpu
from jax.sharding import PartitionSpec as P

LEN = 512
EPS = 1e-06
ROPE_BASE = 1000000.0
MASKED = -1e30
LOW = jnp.bfloat16
F32 = jnp.float32
VMEM_LIMIT = 58 * 2**20


def dot(a, b, ca=1, cb=0):
    return lax.dot_general(a, b, (((ca,), (cb,)), ((), ())), preferred_element_type=F32)


def inverse_root(v):
    return lax.rsqrt(jnp.mean(v * v, axis=-1, keepdims=True) + EPS)


def norm_back(v, gain, c):
    r = inverse_root(v)
    n = v * r
    e = (1.0 + gain) * c
    return (
        r * (e - n * jnp.mean(e * n, axis=-1, keepdims=True)),
        jnp.sum(c * n, axis=0, keepdims=True),
    )


def rotate(u, cosine, sine):
    half = u.shape[-1] // 2
    a, b = u[:, :half], u[:, half:]
    return jnp.concatenate([a * cosine - b * sine, b * cosine + a * sine], axis=-1)


def rotate_back(w, cosine, sine):
    half = w.shape[-1] // 2
    a, b = w[:, :half], w[:, half:]
    return jnp.concatenate([a * cosine + b * sine, b * cosine - a * sine], axis=-1)


def call(body, outs, args, flops):
    return pl.pallas_call(
        body,
        out_shape=[jax.ShapeDtypeStruct(shape, kind) for shape, kind in outs],
        in_specs=[pl.BlockSpec(memory_space=pltpu.VMEM)] * len(args),
        out_specs=[pl.BlockSpec(memory_space=pltpu.VMEM)] * len(outs),
        compiler_params=pltpu.CompilerParams(vmem_limit_bytes=VMEM_LIMIT),
        cost_estimate=pl.CostEstimate(
            flops=flops,
            bytes_accessed=sum(a.size * a.dtype.itemsize for a in args),
            transcendentals=0,
        ),
    )(*args)


def attend_kernel(
    hidden, pre_attention, query_norm, key_norm, kw, vw, q0, q1, q2, q3, cosine, sine,
    seg_col, seg_row, normed_in, query_proj, key_proj, query_rot, key_rot, value_low,
    prob_low, mixture,
):
    h = hidden[...].astype(F32)
    x = (h * inverse_root(h) * (1.0 + pre_attention[...])).astype(LOW)
    normed_in[...] = x
    cos, sin = cosine[...], sine[...]
    k = dot(x, kw[...])
    key_proj[...] = k
    k = rotate(k * inverse_root(k) * (1.0 + key_norm[...]), cos, sin).astype(LOW)
    key_rot[...] = k
    v = dot(x, vw[...]).astype(LOW)
    value_low[...] = v
    scale = k.shape[-1] ** (-0.5)
    shape = (x.shape[0], x.shape[0])
    allowed = (seg_col[...] == seg_row[...]) & (
        lax.broadcasted_iota(jnp.int32, shape, 1) <= lax.broadcasted_iota(jnp.int32, shape, 0)
    )
    for r, qw in enumerate((q0, q1, q2, q3)):
        q = dot(x, qw[...])
        query_proj[r] = q
        q = rotate(q * inverse_root(q) * (1.0 + query_norm[...]), cos, sin).astype(LOW)
        query_rot[r] = q
        s = jnp.where(allowed, dot(q, k, 1, 1) * scale, MASKED)
        e = jnp.exp(s - jnp.max(s, axis=-1, keepdims=True))
        p = (e / jnp.sum(e, axis=-1, keepdims=True)).astype(LOW)
        prob_low[r] = p
        mixture[r] = dot(p, v).astype(LOW)


def middle_kernel(
    hidden, mixture, post_attention, pre_feedforward, o0, o1, o2, o3, attention, middle, normed_mid
):
    total = dot(mixture[0], o0[...])
    for r, ow in ((1, o1), (2, o2), (3, o3)):
        total = total + dot(mixture[r], ow[...])
    attention[...] = total
    m = hidden[...].astype(F32) + total * inverse_root(total) * (1.0 + post_attention[...])
    middle[...] = m
    normed_mid[...] = (m * inverse_root(m) * (1.0 + pre_feedforward[...])).astype(LOW)


GELU_A = 0.7978845608
GELU_B = 0.044715


def feed_kernel(
    attention, middle, normed_mid, cotangent, post_attention, pre_feedforward, post_feedforward,
    g0, g1, g2, g3, u0, u1, u2, u3, d0, d1, d2, d3,
    hidden_out, product_low, feed_grad_low, gate_grad_low, up_grad_low, middle_grad,
    attention_grad_low, grad_norms, gate_keep, up_keep,
):
    x = normed_mid[...]
    feed = None
    for r, (gw, uw, dw) in enumerate(((g0, u0, d0), (g1, u1, d1), (g2, u2, d2), (g3, u3, d3))):
        g = dot(x, gw[...])
        u = dot(x, uw[...])
        t = jnp.tanh(GELU_A * (g + GELU_B * (g * g * g)))
        act = 0.5 * g * (1.0 + t)
        slope = 0.5 * (1.0 + t) + 0.5 * g * (1.0 - t * t) * (
            GELU_A * (1.0 + 3.0 * GELU_B * g * g)
        )
        gate_keep[r] = u * slope
        up_keep[r] = act
        p = (act * u).astype(LOW)
        product_low[r] = p
        part = dot(p, dw[...])
        feed = part if feed is None else feed + part
    m = middle[...]
    hidden_out[...] = (m + feed * inverse_root(feed) * (1.0 + post_feedforward[...])).astype(LOW)
    c = cotangent[...].astype(F32)
    fg, grad_norms[0:1] = norm_back(feed, post_feedforward[...], c)
    fg = fg.astype(LOW)
    feed_grad_low[...] = fg
    total = None
    for r, (gw, uw, dw) in enumerate(((g0, u0, d0), (g1, u1, d1), (g2, u2, d2), (g3, u3, d3))):
        pg = dot(fg, dw[...], 1, 1)
        gg = (pg * gate_keep[r]).astype(LOW)
        ug = (pg * up_keep[r]).astype(LOW)
        gate_grad_low[r] = gg
        up_grad_low[r] = ug
        part = dot(gg, gw[...], 1, 1) + dot(ug, uw[...], 1, 1)
        total = part if total is None else total + part
    back, grad_norms[1:2] = norm_back(m, pre_feedforward[...], total)
    mg = c + back
    middle_grad[...] = mg
    ag, grad_norms[2:3] = norm_back(attention[...], post_attention[...], mg)
    attention_grad_low[...] = ag.astype(LOW)


def outer_units_kernel(a, b, keep, send):
    for r in range(4):
        out = (keep, send)[r % 2]
        out[r // 2] = dot(a[r], b[...], 0, 0).astype(LOW)


def outer_columns_kernel(a, b, keep, send):
    for r in range(4):
        out = (keep, send)[r % 2]
        out[r // 2] = dot(a[...], b[r], 0, 0).astype(LOW)


def attend_back_kernel(
    hidden, middle_grad, attention_grad_low, normed_in, query_proj, key_proj, query_rot, key_rot,
    value_low, prob_low, pre_attention, query_norm, key_norm, cosine, sine, kw, vw,
    q0, q1, q2, q3, o0, o1, o2, o3,
    grad_input, query_keep, query_send, grad_key, grad_value, grad_pre, grad_query_norm,
    grad_key_norm,
):
    cos, sin = cosine[...], sine[...]
    ag = attention_grad_low[...]
    x = normed_in[...]
    k = key_rot[...]
    v = value_low[...]
    scale = k.shape[-1] ** (-0.5)
    key_total = value_total = part = norm_total = None
    for r, (qw, ow) in enumerate(((q0, o0), (q1, o1), (q2, o2), (q3, o3))):
        mg = dot(ag, ow[...], 1, 1).astype(LOW)
        p = prob_low[r]
        pg = dot(mg, v, 1, 1)
        pf = p.astype(F32)
        s = (pf * (pg - jnp.sum(pf * pg, axis=-1, keepdims=True))).astype(LOW)
        qg = dot(s, k) * scale
        kg = dot(s, query_rot[r], 0, 0)
        vg = dot(p, mg, 0, 0)
        qg, gn = norm_back(query_proj[r], query_norm[...], rotate_back(qg, cos, sin))
        qg = qg.astype(LOW)
        out = (query_keep, query_send)[r % 2]
        out[r // 2] = dot(x, qg, 0, 0).astype(LOW)
        ip = dot(qg, qw[...], 1, 1)
        if r == 0:
            key_total, value_total, part, norm_total = kg, vg, ip, gn
        else:
            key_total = key_total + kg
            value_total = value_total + vg
            part = part + ip
            norm_total = norm_total + gn
    grad_query_norm[...] = norm_total
    kg, grad_key_norm[...] = norm_back(
        key_proj[...], key_norm[...], rotate_back(key_total * scale, cos, sin)
    )
    kg = kg.astype(LOW)
    vg = value_total.astype(LOW)
    grad_key[...] = dot(x, kg, 0, 0).astype(LOW)
    grad_value[...] = dot(x, vg, 0, 0).astype(LOW)
    part = part + dot(kg, kw[...], 1, 1) + dot(vg, vw[...], 1, 1)
    back, grad_pre[...] = norm_back(hidden[...].astype(F32), pre_attention[...], part)
    grad_input[...] = (middle_grad[...] + back).astype(LOW)


def swap(array, axis, count, bit):
    return lax.ppermute(array, axis, [(i, i ^ bit) for i in range(count)])


def add_low(a, b):
    return (a.astype(F32) + b.astype(F32)).astype(LOW)


def reduce_shards(keep, send, groups):
    merged = add_low(keep, swap(send, "tensor", 4, 1))
    own = add_low(merged[0], swap(merged[1], "tensor", 4, 2))
    me = lax.axis_index("dp")
    bits = []
    bit = 1
    while bit < groups:
        bits.append(bit)
        bit *= 2
    for bit in bits:
        high = (me // bit) % 2
        half = own.shape[0] // 2
        mine = lax.dynamic_slice_in_dim(own, high * half, half, 0)
        theirs = lax.dynamic_slice_in_dim(own, (1 - high) * half, half, 0)
        own = add_low(mine, swap(theirs, "dp", groups, bit))
    for bit in reversed(bits):
        high = (me // bit) % 2
        other = swap(own, "dp", groups, bit)
        own = jnp.where(
            high == 0,
            jnp.concatenate([own, other], axis=0),
            jnp.concatenate([other, own], axis=0),
        )
    return own


def on_device(groups):
    def run(
        hidden_in, query_weight, key_weight, value_weight, output_weight, gate_weight, up_weight,
        down_weight, pre_attention, query_norm, key_norm, post_attention, pre_feedforward,
        post_feedforward, segments, positions, cotangent,
    ):
        me = lax.axis_index("tensor")
        start = me * LEN
        width, head = key_weight.shape
        units = gate_weight.shape[1]

        def gathered(w):
            w2 = swap(w, "tensor", 4, 2)
            return [w, swap(w, "tensor", 4, 1), w2, swap(w2, "tensor", 4, 1)]

        queries = gathered(query_weight)
        outputs = gathered(output_weight)
        gates = gathered(gate_weight)
        ups = gathered(up_weight)
        downs = gathered(down_weight)

        hidden = lax.dynamic_slice_in_dim(hidden_in, start, LEN, 0)
        cot = lax.dynamic_slice_in_dim(cotangent, start, LEN, 0)
        segment = lax.dynamic_slice_in_dim(segments, start, LEN, 0)
        position = lax.dynamic_slice_in_dim(positions, start, LEN, 0)
        steps = jnp.arange(head // 2).astype(F32)
        frequency = jnp.power(F32(ROPE_BASE), -2.0 * steps / head)
        angles = position.astype(F32)[:, None] * frequency[None, :]
        cosine, sine = jnp.cos(angles), jnp.sin(angles)
        row = lambda v: v.reshape(1, -1)
        pre_a, pre_f = row(pre_attention), row(pre_feedforward)
        post_a, post_f = row(post_attention), row(post_feedforward)
        qn, kn = row(query_norm), row(key_norm)

        normed_in, query_proj, key_proj, query_rot, key_rot, value_low, prob_low, mixture = call(
            attend_kernel,
            [
                ((LEN, width), LOW), ((4, LEN, head), F32), ((LEN, head), F32),
                ((4, LEN, head), LOW), ((LEN, head), LOW), ((LEN, head), LOW),
                ((4, LEN, LEN), LOW), ((4, LEN, head), LOW),
            ],
            [
                hidden, pre_a, qn, kn, key_weight, value_weight, *queries, cosine, sine,
                segment[:, None], segment[None, :],
            ],
            4 * 10**9,
        )
        attention, middle, normed_mid = call(
            middle_kernel,
            [((LEN, width), F32), ((LEN, width), F32), ((LEN, width), LOW)],
            [hidden, mixture, post_a, pre_f, *outputs],
            10**9,
        )
        args = [attention, middle, normed_mid, cot, post_a, pre_f, post_f, *gates, *ups, *downs]
        outs = [
            ((LEN, width), LOW), ((4, LEN, units), LOW), ((LEN, width), LOW),
            ((4, LEN, units), LOW), ((4, LEN, units), LOW), ((LEN, width), F32),
            ((LEN, width), LOW), ((8, width), F32),
        ]
        (
            hidden_out, product_low, feed_grad_low, gate_grad_low, up_grad_low, middle_grad,
            attention_grad_low, grad_norms,
        ) = pl.pallas_call(
            feed_kernel,
            out_shape=[jax.ShapeDtypeStruct(shape, kind) for shape, kind in outs],
            in_specs=[pl.BlockSpec(memory_space=pltpu.VMEM)] * len(args),
            out_specs=[pl.BlockSpec(memory_space=pltpu.VMEM)] * len(outs),
            scratch_shapes=[pltpu.VMEM((4, LEN, units), F32)] * 2,
            compiler_params=pltpu.CompilerParams(vmem_limit_bytes=VMEM_LIMIT),
            cost_estimate=pl.CostEstimate(
                flops=10**10, bytes_accessed=2 * 10**7, transcendentals=0
            ),
        )(*args)
        hidden_out = lax.all_gather(hidden_out, "tensor", tiled=True)

        def outer(body, a, b, shape):
            return call(body, [((2, *shape), LOW)] * 2, [a, b], 14 * 10**8)

        down = outer(outer_units_kernel, product_low, feed_grad_low, (units, width))
        gate = outer(outer_columns_kernel, normed_mid, gate_grad_low, (width, units))
        up = outer(outer_columns_kernel, normed_mid, up_grad_low, (width, units))
        output = outer(outer_units_kernel, mixture, attention_grad_low, (head, width))
        (
            grad_input, query_keep, query_send, grad_key, grad_value, grad_pre, grad_qn, grad_kn,
        ) = call(
            attend_back_kernel,
            [
                ((LEN, width), LOW), ((2, width, head), LOW), ((2, width, head), LOW),
                ((width, head), LOW), ((width, head), LOW), ((1, width), F32), ((1, head), F32),
                ((1, head), F32),
            ],
            [
                hidden, middle_grad, attention_grad_low, normed_in, query_proj, key_proj,
                query_rot, key_rot, value_low, prob_low, pre_a, qn, kn, cosine, sine, key_weight,
                value_weight, *queries, *outputs,
            ],
            6 * 10**9,
        )
        grad_input = lax.all_gather(grad_input, "tensor", tiled=True).astype(F32)

        small = jnp.concatenate(
            [grad_norms[:3].reshape(-1), grad_pre[0], grad_qn[0], grad_kn[0]]
        ).astype(LOW)
        quarter = (2 * width + 256) // 4
        small = jnp.pad(small, (0, 256 * head - small.shape[0])).reshape(256, head)
        shared = jnp.concatenate([grad_key, grad_value, small], axis=0)
        parts = [
            lax.dynamic_slice_in_dim(shared, (me ^ r) * quarter, quarter, 0) for r in range(4)
        ]
        keep = jnp.concatenate([query_keep, jnp.stack([parts[0], parts[2]])], axis=1)
        send = jnp.concatenate([query_send, jnp.stack([parts[1], parts[3]])], axis=1)

        grad_down = reduce_shards(*down, groups).astype(F32)
        grad_gate = reduce_shards(*gate, groups).astype(F32)
        grad_up = reduce_shards(*up, groups).astype(F32)
        grad_output = reduce_shards(*output, groups).astype(F32)
        last = reduce_shards(keep, send, groups)
        grad_query = last[:width].astype(F32)
        shared = lax.all_gather(last[width:], "tensor", tiled=True).astype(F32)
        small = shared[2 * width :].reshape(-1)
        cuts = [0]
        for size in (width, width, width, width, head, head):
            cuts.append(cuts[-1] + size)
        post_f, pre_f, post_a, pre_a, qn, kn = [
            small[a:b] for a, b in zip(cuts[:-1], cuts[1:])
        ]
        return (
            hidden_out, grad_input, grad_query, shared[:width], shared[width : 2 * width],
            grad_output, grad_gate, grad_up, grad_down, pre_a, qn, kn, post_a, pre_f, post_f,
        )

    return run


def solution(mesh):
    placed = (
        P("dp", None), P(None, "tensor"), P(), P(), P("tensor", None), P(None, "tensor"),
        P(None, "tensor"), P("tensor", None), P(), P(), P(), P(), P(), P(), P("dp"), P("dp"),
        P("dp", None),
    )
    return jax.shard_map(
        on_device(mesh.shape["dp"]),
        mesh=mesh,
        in_specs=placed,
        out_specs=(
            P("dp", None), P("dp", None), P(None, "tensor"), P(), P(), P("tensor", None),
            P(None, "tensor"), P(None, "tensor"), P("tensor", None), P(), P(), P(), P(), P(), P(),
        ),
        check_vma=False,
    )
```

time: 920 us -> 320 us (0.35)
  waiting for transfers between devices: 502 us -> 132 us
  local copies, waits for them, and re-layouts: 153 us -> 18.9 us
  matrix products: 95.9 us -> 0 us
  blocking collectives: 77.9 us -> 10.4 us
  Pallas kernels: 0 us -> 64.1 us
  starting transfers between devices: 0.88 us -> 54.6 us
  other arithmetic: 64 us -> 21.4 us
    psum x6 -> x0, waiting for transfers between devices: 502 us -> none  [the longest x1 190 us: on_device(): lax.psum((grad_query_weight, grad_output_weight, grad_gate_weight, grad_u...]
    ppermute x0 -> x55, waiting for transfers between devices: none -> 132 us  [swap(): return lax.ppermute(array, axis, [(i, i ^ bit) for i in range(count)])]
    dynamic_update_slice x36 -> x0, local copies, waits for them, and re-layouts: 106 us -> none  [the longest x16 92.6 us: run_layer(): lax.map(attend_back, (query_packs, key_packs, value_packs, segment_packs,...]
    dot_general x49 -> x0, matrix products: 95.9 us -> none  [the longest x8 11.7 us: pack_scores(): jnp.einsum('ihd,jd->hij', queries, key_rows, preferred_element_type=jnp.f...]
    psum x2 -> x0, blocking collectives: 77.9 us -> none  [the longest x1 40.2 us: on_device(): lax.psum((grad_key_weight, grad_value_weight, grad_query_norm, grad_key_n...]
    pallas_call x0 -> x8, Pallas kernels: none -> 64.1 us  [the longest x7 44.4 us: call(): pl.pallas_call(body, out_shape=[jax.ShapeDtypeStruct(shape, kind) for sha...]
    ppermute x0 -> x55, starting transfers between devices: none -> 54.5 us  [swap(): return lax.ppermute(array, axis, [(i, i ^ bit) for i in range(count)])]
    reduce_sum x15 -> x0, other arithmetic: 32.4 us -> none  [the longest x6 21.5 us: normed(): return values * inverse * (1.0 + norm_gain)]
  transfers between devices with their start and end apart: 6 -> 57, of which waited for: 6 -> 26; matrix products, arithmetic and copies ran while one was open for 3% -> 11% of each run, Pallas kernels for 0% -> 10%
where the time goes in v1:
time: 320 us; the launch traced here: 317 us
  waiting for transfers between devices  132 us (41%)
  Pallas kernels  64.1 us (20%)
  starting transfers between devices  54.6 us (17%)
  other arithmetic  21.4 us (7%)
  local copies, waits for them, and re-layouts  18.9 us (6%)
  between operations  15.2 us (5%)
  blocking collectives  10.4 us (3%)
    ppermute x55, waiting for transfers between devices, swap(): return lax.ppermute(array, axis, [(i, i ^ bit) for i in range(count)])  132 us
    ppermute x55, starting transfers between devices, swap(): return lax.ppermute(array, axis, [(i, i ^ bit) for i in range(count)])  54.5 us
    pallas_call x7, Pallas kernels, call(): pl.pallas_call(body, out_shape=[jax.ShapeDtypeStruct(shape, kind) for sha...  44.4 us
    pallas_call x1, Pallas kernels, run(): pl.pallas_call(feed_kernel, out_shape=[jax.ShapeDtypeStruct(shape, kind)...  19.6 us
    all_gather x1, blocking collectives, run(): shared = lax.all_gather(last[width:], 'tensor', tiled=True).astype(F32)  10.4 us
    convert_element_type x25, other arithmetic, add_low(): return (a.astype(F32) + b.astype(F32)).astype(LOW)  6.77 us
  transfers between devices with their start and end apart: 57, of which 26 were waited for; matrix products, arithmetic and copies ran while one was open for 11% of the time, Pallas kernels for 10%

profile of v1, /device:TPU:0, one launch (start us, length us, event | category | flops | bytes accessed | tf_op | source)
XLA Modules:
  0.0 316.6 jit_solution(2039931312553396464)
XLA Ops:
  10.8 8.3 %collective-permute-done.1.q2 = bf16[640,256]{1,0:T(8,128)(2,1)} collective-permute-done((bf16[640,256]{1,0:T(8,128)(2,1)}, bf16[640,256]{1,0:T(8,128)(2,1)}, u32[]{:S(2)}, u32[]{:S(2)}) %collective-permute-start.1) | collective-permute-done | bytes 327712 | tf_op jit(solution)/shard_map/ppermute | solution.py:215
  21.3 4.9 %collective-permute-done.4.o2 = bf16[256,640]{1,0:T(8,128)(2,1)} collective-permute-done((bf16[256,640]{1,0:T(8,128)(2,1)}, bf16[256,640]{1,0:T(8,128)(2,1)}, u32[]{:S(2)}, u32[]{:S(2)}) %collective-permute-start.4) | collective-permute-done | bytes 327712 | tf_op jit(solution)/shard_map/ppermute | solution.py:215
  40.1 14.1 %collective-permute-done.13.d2 = bf16[512,640]{1,0:T(8,128)(2,1)} collective-permute-done((bf16[512,640]{1,0:T(8,128)(2,1)}, bf16[512,640]{1,0:T(8,128)(2,1)}, u32[]{:S(2)}, u32[]{:S(2)}) %collective-permute-start.13) | collective-permute-done | bytes 655392 | tf_op jit(solution)/shard_map/ppermute | solution.py:215
  54.2 13.2 %collective-permute-done.7.g2 = bf16[640,512]{1,0:T(8,128)(2,1)} collective-permute-done((bf16[640,512]{1,0:T(8,128)(2,1)}, bf16[640,512]{1,0:T(8,128)(2,1)}, u32[]{:S(2)}, u32[]{:S(2)}) %collective-permute-start.7) | collective-permute-done | bytes 655392 | tf_op jit(solution)/shard_map/ppermute | solution.py:215
  69.9 8.3 %shard_map.280 = (bf16[512,640]{1,0:T(8,128)(2,1)}, f32[4,512,256]{2,1,0:T(8,128)}, f32[512,256]{1,0:T(8,128)}, bf16[4,512,256]{2,1,0:T(8,128)(2,1)}, bf16[512,2...) custom-call(bf16[512,640]{1,0:T(8,128)(2,1)} %constant_dynamic-slice_fus, ...), custom_call_target="tpu_custom_call" | custom-call | flops 4000000000 | bytes 3154432 | tf_op jit(solution)/shard_map/pallas_call | solution.py:48
  78.3 4.5 %shard_map.281 = (f32[512,640]{1,0:T(8,128)}, f32[512,640]{1,0:T(8,128)}, bf16[512,640]{1,0:T(8,128)(2,1)}) custom-call(bf16[512,640]{1,0:T(8,128)(2,1)} %constant_dynamic-slice_fusion.16.hidden, bf16[4,512,256]{2,1,0:T(8,128)(2,1)} %get-tuple-element.50.mixture.a, f32[1,640]{1,0:T(1,128)} %reshape.80.post_attention, f32[1,640]{1,0:T(1,128)} %reshape.81.pre_feedforward, ...), custom_call_target="tpu_custom_call" | custom-call | flops 1000000000 | bytes 3019776 | tf_op jit(solution)/shard_map/pallas_call | solution.py:48
  84.5 19.6 %shard_map.282 = (bf16[512,640]{1,0:T(8,128)(2,1)}, bf16[4,512,512]{2,1,0:T(8,128)(2,1)}, bf16[512,640]{1,0:T(8,128)(2,1)}, bf16[4,512,512]{2,1,0:T(8,128)(2,1)}...) custom-call(f32[512,640]{1,0:T(8,128)} %get-tuple-element.51.attention, ...), custom_call_target="tpu_custom_call" | custom-call | flops 10000000000 | bytes 20000000 | tf_op jit(solution)/shard_map/pallas_call | solution.py:310
  104.1 14.0 %shard_map.283 = (bf16[512,640]{1,0:T(8,128)(2,1)}, bf16[2,640,256]{2,1,0:T(8,128)(2,1)}, bf16[2,640,256]{2,1,0:T(8,128)(2,1)}, bf16[640,256]{1,0:T(8,128)(2,1)}...) custom-call(bf16[512,640]{1,0:T(8,128)(2,1)} %constant_dynamic-slice_fusion.16.hidden, ...), custom_call_target="tpu_custom_call" | custom-call | flops 6000000000 | bytes 13373952 | tf_op jit(solution)/shard_map/pallas_call | solution.py:48
  127.3 5.2 %shard_map.287 = (bf16[2,512,640]{2,1,0:T(8,128)(2,1)}, bf16[2,512,640]{2,1,0:T(8,128)(2,1)}) custom-call(bf16[4,512,512]{2,1,0:T(8,128)(2,1)} %get-tuple-element.81.a, bf16[512,640]{1,0:T(8,128)(2,1)} %get-tuple-element.82.b), custom_call_target="tpu_custom_call" | custom-call | flops 1400000000 | bytes 2752512 | tf_op jit(solution)/shard_map/pallas_call | solution.py:48
  132.8 7.3 %collective-permute-done.24 = bf16[256,640]{1,0:T(8,128)(2,1)S(1)} collective-permute-done((bf16[256,640]{1,0:T(8,128)(2,1)S(1)}, bf16[256,640]{1,0:T(8,128)(2,1)S(1)}, u32[]{:S(2)}, u32[]{:S(2)}) %collective-permute-start.24) | collective-permute-done | bytes 327712 | tf_op jit(solution)/shard_map/ppermute | solution.py:215
  141.6 4.5 %shard_map.286 = (bf16[2,640,512]{2,1,0:T(8,128)(2,1)}, bf16[2,640,512]{2,1,0:T(8,128)(2,1)}) custom-call(bf16[512,640]{1,0:T(8,128)(2,1)} %get-tuple-element.53.normed_mid.a, bf16[4,512,512]{2,1,0:T(8,128)(2,1)} %get-tuple-element.78.b), custom_call_target="tpu_custom_call" | custom-call | flops 1400000000 | bytes 2752512 | tf_op jit(solution)/shard_map/pallas_call | solution.py:48
  146.1 4.5 %shard_map.285 = (bf16[2,640,512]{2,1,0:T(8,128)(2,1)}, bf16[2,640,512]{2,1,0:T(8,128)(2,1)}) custom-call(bf16[512,640]{1,0:T(8,128)(2,1)} %get-tuple-element.53.normed_mid.a, bf16[4,512,512]{2,1,0:T(8,128)(2,1)} %get-tuple-element.75.b), custom_call_target="tpu_custom_call" | custom-call | flops 1400000000 | bytes 2752512 | tf_op jit(solution)/shard_map/pallas_call | solution.py:48
  174.8 10.4 %collective-permute-done.16 = bf16[1024,256]{1,0:T(8,128)(2,1)S(1)} collective-permute-done((bf16[1024,256]{1,0:T(8,128)(2,1)S(1)}, bf16[1024,256]{1,0:T(8,128)(2,1)S(1)}, u32[]{:S(2)}, u32[]{:S(2)}) %collective-permute-start.16) | collective-permute-done | bytes 524320 | tf_op jit(solution)/shard_map/ppermute | solution.py:215
  193.7 8.5 %collective-permute-done.48 = bf16[512,640]{1,0:T(8,128)(2,1)S(1)} collective-permute-done((bf16[512,640]{1,0:T(8,128)(2,1)S(1)}, bf16[512,640]{1,0:T(8,128)(2,1)S(1)}, u32[]{:S(2)}, u32[]{:S(2)}) %collective-permute-start.48) | collective-permute-done | bytes 655392 | tf_op jit(solution)/shard_map/ppermute | solution.py:215
  203.5 12.7 %collective-permute-done.40 = bf16[640,512]{1,0:T(8,128)(2,1)S(1)} collective-permute-done((bf16[640,512]{1,0:T(8,128)(2,1)S(1)}, bf16[640,512]{1,0:T(8,128)(2,1)S(1)}, u32[]{:S(2)}, u32[]{:S(2)}) %collective-permute-start.40) | collective-permute-done | bytes 655392 | tf_op jit(solution)/shard_map/ppermute | solution.py:215
  217.5 4.1 %collective-permute-done.20 = bf16[128,256]{1,0:T(8,128)(2,1)S(1)} collective-permute-done((bf16[128,256]{1,0:T(8,128)(2,1)S(1)}, bf16[128,256]{1,0:T(8,128)(2,1)S(1)}, u32[]{:S(2)}, u32[]{:S(2)}) %collective-permute-start.20) | collective-permute-done | bytes 65568 | tf_op jit(solution)/shard_map/ppermute | solution.py:215
  223.3 4.7 %collective-permute-done.32 = bf16[640,512]{1,0:T(8,128)(2,1)S(1)} collective-permute-done((bf16[640,512]{1,0:T(8,128)(2,1)S(1)}, bf16[640,512]{1,0:T(8,128)(2,1)S(1)}, u32[]{:S(2)}, u32[]{:S(2)}) %collective-permute-start.32) | collective-permute-done | bytes 655392 | tf_op jit(solution)/shard_map/ppermute | solution.py:215
  232.9 5.9 %collective-permute-done.33 = bf16[320,512]{1,0:T(8,128)(2,1)S(1)} collective-permute-done((bf16[320,512]{1,0:T(8,128)(2,1)S(1)}, bf16[320,512]{1,0:T(8,128)(2,1)S(1)}, u32[]{:S(2)}, u32[]{:S(2)}) %collective-permute-start.33) | collective-permute-done | bytes 327712 | tf_op jit(solution)/shard_map/ppermute | solution.py:215
  245.0 10.4 %all_gather.11 = bf16[1536,256]{1,0:T(8,128)(2,1)S(1)} all-gather(bf16[384,256]{1,0:T(8,128)(2,1)S(1)} %slice.103), channel_id=1, replica_groups=mesh['dp'=8,'tensor'=4] {'tensor'}, dimensions={0}, use_global_device_ids=true | all-gather | bytes 983040 | tf_op jit(solution)/shard_map/all_gather | solution.py:366
  264.4 5.2 %collective-permute-done.52 = bf16[64,640]{1,0:T(8,128)(2,1)S(1)} collective-permute-done((bf16[64,640]{1,0:T(8,128)(2,1)S(1)}, bf16[64,640]{1,0:T(8,128)(2,1)S(1)}, u32[]{:S(2)}, u32[]{:S(2)}) %collective-permute-start.52) | collective-permute-done | bytes 81952 | tf_op jit(solution)/shard_map/ppermute | solution.py:215
  288.8 5.8 %collective-permute-done.46 = bf16[320,512]{1,0:T(8,128)(2,1)S(1)} collective-permute-done((bf16[320,512]{1,0:T(8,128)(2,1)S(1)}, bf16[320,512]{1,0:T(8,128)(2,1)S(1)}, u32[]{:S(2)}, u32[]{:S(2)}) %collective-permute-start.46) | collective-permute-done | bytes 327712 | tf_op jit(solution)/shard_map/ppermute | solution.py:215
  295.8 4.4 %collective-permute-done.38 = bf16[320,512]{1,0:T(8,128)(2,1)S(1)} collective-permute-done((bf16[320,512]{1,0:T(8,128)(2,1)S(1)}, bf16[320,512]{1,0:T(8,128)(2,1)S(1)}, u32[]{:S(2)}, u32[]{:S(2)}) %collective-permute-start.38) | collective-permute-done | bytes 327712 | tf_op jit(solution)/shard_map/ppermute | solution.py:215
  301.4 4.4 %convert_element_type.276 = f32[2048,640]{1,0:T(8,128)} convert(bf16[2048,640]{1,0:T(8,128)(2,1)} %all-gather.5.cloned.1.call-done) | non-fusion elementwise | flops 1310720 | bytes 7864320 | tf_op jit(solution)/shard_map/convert_element_type | solution.py:346
  305.9 3.6 %copy.37 = bf16[2048,640]{1,0:T(8,128)(2,1)} copy(bf16[2048,640]{1,0:T(8,128)(2,1)} %all-gather.3.cloned.1.call-done) | data formatting | bytes 5242880
  (237 shorter events, 112.7 us)
Async XLA Ops:
  7.2 294.2 %all-gather.5.cloned.1.call-start = ((), (), s32[]{:S(2)}) async-start(), calls=%async_computation.1 | async-start | bytes 3276800 | tf_op jit(solution)/shard_map/all_gather | solution.py:346
  10.4 17.8 %collective-permute-start.3 = (bf16[256,640]{1,0:T(8,128)(2,1)}, bf16[256,640]{1,0:T(8,128)(2,1)}, u32[]{:S(2)}, u32[]{:S(2)}) collective-permute-start(bf16[256,640]{1,0:T(8,128)(2,1)} %o0.3), channel_id=1, source_target_pairs={{0,1},{1,0},{2,3},{3,2},{4,5},{5,4},{6,7},{7,6},{8,9},{9,8},{10,11... | collective-permute-start | bytes 983048 | tf_op jit(solution)/shard_map/ppermute | solution.py:215
  19.1 16.5 %collective-permute-start.2 = (bf16[640,256]{1,0:T(8,128)(2,1)}, bf16[640,256]{1,0:T(8,128)(2,1)}, u32[]{:S(2)}, u32[]{:S(2)}) collective-permute-start(bf16[640,256]{1,0:T(8,128)(2,1)} %collective-permute-done.1.q2), channel_id=1, source_target_pairs={{0,1},{1,0},{2,3},{3,2},{4,5},{5,4},{6,7},{7,6},{8,9},{9,8},{10,11... | collective-permute-start | bytes 983048 | tf_op jit(solution)/shard_map/ppermute | solution.py:215
  19.1 21.0 %collective-permute-start.10 = (bf16[640,512]{1,0:T(8,128)(2,1)}, bf16[640,512]{1,0:T(8,128)(2,1)S(1)}, u32[]{:S(2)}, u32[]{:S(2)}) collective-permute-start(bf16[640,512]{1,0:T(8,128)(2,1)} %u0.1), channel_id=1, source_target_pairs={{0,2},{1,3},{2,0},{3,1},{4,6},{5,7},{6,4},{7,5},{8,10},{9,11},{10,... | collective-permute-start | bytes 1966088 | tf_op jit(solution)/shard_map/ppermute | solution.py:215
  21.2 33.0 %collective-permute-start.13 = (bf16[512,640]{1,0:T(8,128)(2,1)}, bf16[512,640]{1,0:T(8,128)(2,1)}, u32[]{:S(2)}, u32[]{:S(2)}) collective-permute-start(bf16[512,640]{1,0:T(8,128)(2,1)} %d0.1), channel_id=1, source_target_pairs={{0,2},{1,3},{2,0},{3,1},{4,6},{5,7},{6,4},{7,5},{8,10},{9,11},{10,... | collective-permute-start | bytes 1966088 | tf_op jit(solution)/shard_map/ppermute | solution.py:215
  26.2 41.3 %collective-permute-start.7 = (bf16[640,512]{1,0:T(8,128)(2,1)}, bf16[640,512]{1,0:T(8,128)(2,1)}, u32[]{:S(2)}, u32[]{:S(2)}) collective-permute-start(bf16[640,512]{1,0:T(8,128)(2,1)} %g0.1), channel_id=1, source_target_pairs={{0,2},{1,3},{2,0},{3,1},{4,6},{5,7},{6,4},{7,5},{8,10},{9,11},{10,... | collective-permute-start | bytes 1966088 | tf_op jit(solution)/shard_map/ppermute | solution.py:215
  28.2 39.3 %collective-permute-start.12 = (bf16[512,640]{1,0:T(8,128)(2,1)}, bf16[512,640]{1,0:T(8,128)(2,1)}, u32[]{:S(2)}, u32[]{:S(2)}) collective-permute-start(bf16[512,640]{1,0:T(8,128)(2,1)} %d0.1), channel_id=1, source_target_pairs={{0,1},{1,0},{2,3},{3,2},{4,5},{5,4},{6,7},{7,6},{8,9},{9,8},{10,11... | collective-permute-start | bytes 1966088 | tf_op jit(solution)/shard_map/ppermute | solution.py:215
  39.1 43.7 %collective-permute-start.6 = (bf16[640,512]{1,0:T(8,128)(2,1)S(1)}, bf16[640,512]{1,0:T(8,128)(2,1)S(1)}, u32[]{:S(2)}, u32[]{:S(2)}) collective-permute-start(bf16[640,512]{1,0:T(8,128)(2,1)S(1)} %copy-done.14), channel_id=1, source_target_pairs={{0,1},{1,0},{2,3},{3,2},{4,5},{5,4},{6,7},{7,6},{8,9},{9,8},{10,11... | collective-permute-start | bytes 1966088 | tf_op jit(solution)/shard_map/ppermute | solution.py:215
  40.1 42.7 %collective-permute-start.9 = (bf16[640,512]{1,0:T(8,128)(2,1)S(1)}, bf16[640,512]{1,0:T(8,128)(2,1)S(1)}, u32[]{:S(2)}, u32[]{:S(2)}) collective-permute-start(bf16[640,512]{1,0:T(8,128)(2,1)S(1)} %copy-done.15), channel_id=1, source_target_pairs={{0,1},{1,0},{2,3},{3,2},{4,5},{5,4},{6,7},{7,6},{8,9},{9,8},{10,11... | collective-permute-start | bytes 1966088 | tf_op jit(solution)/shard_map/ppermute | solution.py:215
  54.2 28.6 %collective-permute-start.11 = (bf16[640,512]{1,0:T(8,128)(2,1)S(1)}, bf16[640,512]{1,0:T(8,128)(2,1)S(1)}, u32[]{:S(2)}, u32[]{:S(2)}) collective-permute-start(bf16[640,512]{1,0:T(8,128)(2,1)S(1)} %collective-permute-done.10.u2), channel_id=1, source_target_pairs={{0,1},{1,0},{2,3},{3,2},{4,5},{5,4},{6,7},{7,6},{8,9},{9,8},{10,11... | collective-permute-start | bytes 1966088 | tf_op jit(solution)/shard_map/ppermute | solution.py:215
  118.2 187.7 %all-gather.3.cloned.1.call-start = ((), (), s32[]{:S(2)}) async-start(), calls=%async_computation | async-start | bytes 3276800 | tf_op jit(solution)/shard_map/all_gather | solution.py:321
  127.3 25.7 %collective-permute-start.15 = (bf16[2,1024,256]{2,1,0:T(8,128)(2,1)}, bf16[2,1024,256]{2,1,0:T(8,128)(2,1)}, u32[]{:S(2)}, u32[]{:S(2)}) collective-permute-start(bf16[2,1024,256]{2,1,0:T(8,128)(2,1)} %maximum_maximum_fusion), channel_id=1, source_target_pairs={{0,1},{1,0},{2,3},{3,2},{4,5},{5,4},{6,7},{7,6},{8,9},{9,8},{10,11... | collective-permute-start | bytes 3145736 | tf_op jit(solution)/shard_map/ppermute | solution.py:215
  132.5 31.2 %collective-permute-start.47 = (bf16[2,512,640]{2,1,0:T(8,128)(2,1)}, bf16[2,512,640]{2,1,0:T(8,128)(2,1)S(1)}, u32[]{:S(2)}, u32[]{:S(2)}) collective-permute-start(bf16[2,512,640]{2,1,0:T(8,128)(2,1)} %get-tuple-element.84), channel_id=1, source_target_pairs={{0,1},{1,0},{2,3},{3,2},{4,5},{5,4},{6,7},{7,6},{8,9},{9,8},{10,11... | collective-permute-start | bytes 3932168 | tf_op jit(solution)/shard_map/ppermute | solution.py:215
  146.1 20.5 %collective-permute-start.39 = (bf16[2,640,512]{2,1,0:T(8,128)(2,1)}, bf16[2,640,512]{2,1,0:T(8,128)(2,1)}, u32[]{:S(2)}, u32[]{:S(2)}) collective-permute-start(bf16[2,640,512]{2,1,0:T(8,128)(2,1)} %get-tuple-element.80), channel_id=1, source_target_pairs={{0,1},{1,0},{2,3},{3,2},{4,5},{5,4},{6,7},{7,6},{8,9},{9,8},{10,11... | collective-permute-start | bytes 3932168 | tf_op jit(solution)/shard_map/ppermute | solution.py:215
  150.6 20.9 %collective-permute-start.31 = (bf16[2,640,512]{2,1,0:T(8,128)(2,1)}, bf16[2,640,512]{2,1,0:T(8,128)(2,1)}, u32[]{:S(2)}, u32[]{:S(2)}) collective-permute-start(bf16[2,640,512]{2,1,0:T(8,128)(2,1)} %get-tuple-element.77), channel_id=1, source_target_pairs={{0,1},{1,0},{2,3},{3,2},{4,5},{5,4},{6,7},{7,6},{8,9},{9,8},{10,11... | collective-permute-start | bytes 3932168 | tf_op jit(solution)/shard_map/ppermute | solution.py:215
  158.7 26.5 %collective-permute-start.16 = (bf16[1024,256]{1,0:T(8,128)(2,1)S(1)}, bf16[1024,256]{1,0:T(8,128)(2,1)S(1)}, u32[]{:S(2)}, u32[]{:S(2)}) collective-permute-start(bf16[1024,256]{1,0:T(8,128)(2,1)S(1)} %slice_bitcast_fusion.6), channel_id=1, source_target_pairs={{0,2},{1,3},{2,0},{3,1},{4,6},{5,7},{6,4},{7,5},{8,10},{9,11},{10,... | collective-permute-start | bytes 1572872 | tf_op jit(solution)/shard_map/ppermute | solution.py:215
  164.0 38.1 %collective-permute-start.48 = (bf16[512,640]{1,0:T(8,128)(2,1)S(1)}, bf16[512,640]{1,0:T(8,128)(2,1)S(1)}, u32[]{:S(2)}, u32[]{:S(2)}) collective-permute-start(bf16[512,640]{1,0:T(8,128)(2,1)S(1)} %slice_bitcast_fusion), channel_id=1, source_target_pairs={{0,2},{1,3},{2,0},{3,1},{4,6},{5,7},{6,4},{7,5},{8,10},{9,11},{10,... | collective-permute-start | bytes 1966088 | tf_op jit(solution)/shard_map/ppermute | solution.py:215
  168.3 47.8 %collective-permute-start.40 = (bf16[640,512]{1,0:T(8,128)(2,1)S(1)}, bf16[640,512]{1,0:T(8,128)(2,1)S(1)}, u32[]{:S(2)}, u32[]{:S(2)}) collective-permute-start(bf16[640,512]{1,0:T(8,128)(2,1)S(1)} %slice_bitcast_fusion.2), channel_id=1, source_target_pairs={{0,2},{1,3},{2,0},{3,1},{4,6},{5,7},{6,4},{7,5},{8,10},{9,11},{10,... | collective-permute-start | bytes 1966088 | tf_op jit(solution)/shard_map/ppermute | solution.py:215
  185.5 42.5 %collective-permute-start.32 = (bf16[640,512]{1,0:T(8,128)(2,1)S(1)}, bf16[640,512]{1,0:T(8,128)(2,1)S(1)}, u32[]{:S(2)}, u32[]{:S(2)}) collective-permute-start(bf16[640,512]{1,0:T(8,128)(2,1)S(1)} %slice_bitcast_fusion.4), channel_id=1, source_target_pairs={{0,2},{1,3},{2,0},{3,1},{4,6},{5,7},{6,4},{7,5},{8,10},{9,11},{10,... | collective-permute-start | bytes 1966088 | tf_op jit(solution)/shard_map/ppermute | solution.py:215
  202.3 28.2 %collective-permute-start.49 = (bf16[256,640]{1,0:T(8,128)(2,1)S(1)}, bf16[256,640]{1,0:T(8,128)(2,1)S(1)}, u32[]{:S(2)}, u32[]{:S(2)}) collective-permute-start(bf16[256,640]{1,0:T(8,128)(2,1)S(1)} %constant_dynamic-slice_fusion.2), channel_id=1, source_target_pairs={{0,4},{4,0},{8,12},{12,8},{16,20},{20,16},{24,28},{28,24},{1,5},{5... | collective-permute-start | bytes 983048 | tf_op jit(solution)/shard_map/ppermute | solution.py:215
  240.8 17.5 %collective-permute-start.51 = (bf16[64,640]{1,0:T(8,128)(2,1)S(1)}, bf16[64,640]{1,0:T(8,128)(2,1)S(1)}, u32[]{:S(2)}, u32[]{:S(2)}) collective-permute-start(bf16[64,640]{1,0:T(8,128)(2,1)S(1)} %constant_dynamic-slice_fusion), channel_id=1, source_target_pairs={{0,16},{4,20},{8,24},{12,28},{16,0},{20,4},{24,8},{28,12},{1,17},{... | collective-permute-start | bytes 245768 | tf_op jit(solution)/shard_map/ppermute | solution.py:215
  241.3 20.0 %collective-permute-start.43 = (bf16[80,512]{1,0:T(8,128)(2,1)S(1)}, bf16[80,512]{1,0:T(8,128)(2,1)S(1)}, u32[]{:S(2)}, u32[]{:S(2)}) collective-permute-start(bf16[80,512]{1,0:T(8,128)(2,1)S(1)} %constant_dynamic-slice_fusion.3), channel_id=1, source_target_pairs={{0,16},{4,20},{8,24},{12,28},{16,0},{20,4},{24,8},{28,12},{1,17},{... | collective-permute-start | bytes 245768 | tf_op jit(solution)/shard_map/ppermute | solution.py:215
  244.4 17.0 %collective-permute-start.35 = (bf16[80,512]{1,0:T(8,128)(2,1)S(1)}, bf16[80,512]{1,0:T(8,128)(2,1)S(1)}, u32[]{:S(2)}, u32[]{:S(2)}) collective-permute-start(bf16[80,512]{1,0:T(8,128)(2,1)S(1)} %constant_dynamic-slice_fusion.6), channel_id=1, source_target_pairs={{0,16},{4,20},{8,24},{12,28},{16,0},{20,4},{24,8},{28,12},{1,17},{... | collective-permute-start | bytes 245768 | tf_op jit(solution)/shard_map/ppermute | solution.py:215
  283.7 16.5 %collective-permute-start.38 = (bf16[320,512]{1,0:T(8,128)(2,1)S(1)}, bf16[320,512]{1,0:T(8,128)(2,1)S(1)}, u32[]{:S(2)}, u32[]{:S(2)}) collective-permute-start(bf16[320,512]{1,0:T(8,128)(2,1)S(1)} %maximum_select_fusion.5), channel_id=1, source_target_pairs={{0,4},{4,0},{8,12},{12,8},{16,20},{20,16},{24,28},{28,24},{1,5},{5... | collective-permute-start | bytes 983048 | tf_op jit(solution)/shard_map/ppermute | solution.py:215
  (55 other events, 465.8 us)
Sparse Core Ops, SparseCore 0:
  118.3 31.4 all-gather.4
  151.4 41.0 all-gather.2
